TPU v7x, 32 devices: a whole 2x2x4 slice. The times are simulated.
32 devices in a mesh: row: 4 (over x, core), col: 8 (over z, y).
Axes of the slice: x: 2, y: 2, z: 4, core: 2. Of those that a mesh axis runs over, the one named last changes fastest.
Arguments:
- coefs: bfloat16 [1024, 4096], P('col', 'row'), may hold values from -6 to 6
- direction: bfloat16 [1024, 4096], P('col', 'row'), may hold values from -6 to 6
- tiles: bfloat16 [4, 192, 4096], P('row', 'col'), may hold values from -0.3125 to 0.3125
- block_rows: int32 [4, 192], P('row', 'col'), may hold values from 0 to 15
- block_cols: int32 [4, 192], P('row', 'col'), may hold values from 0 to 63
- counts: int32 [4, 8], P('row', 'col'), may hold values from 3 to 24, as said below
Outputs:
- h_coefs: bfloat16 [1024, 4096], P('col', 'row')
- h_direction: bfloat16 [1024, 4096], P('col', 'row')
Inputs may be any that keep to these rules, and one draw needn't show every extreme that they name: `counts`: each value lies between 3 and 24; some device's list is full in every draw. `block_cols`: tiles of one device may repeat a place.
All inputs are finite; a program needn't handle non-finite values.
Results may differ from a plain program's by a relative error of at most 0.008.
Values may be sent and summed in bfloat16 or wider, within the bound.
A program may use at most 128 MiB of HBM per device.

v0:
```python
import jax
import jax.numpy as jnp
from jax import lax
from jax.sharding import PartitionSpec as P

BLOCK = 64


def make_folder(panels, row_blocks, total, piece):
    targets = lax.iota(jnp.int32, row_blocks)
    tile_flat, tile_rows, tile_cols = piece
    amount = tile_flat.shape[0]
    tile_mats = tile_flat.reshape(amount, BLOCK, BLOCK)
    picked = jnp.take(panels, tile_cols, axis=2)
    contrib = jnp.einsum("pij,sopj->psoi", tile_mats, picked, preferred_element_type=jnp.float32)
    contrib = contrib.reshape(amount, -1)
    upper = contrib.astype(jnp.bfloat16)
    lower = (contrib - upper.astype(jnp.float32)).astype(jnp.bfloat16)
    placing = (targets[:, None] == tile_rows[None, :]).astype(jnp.bfloat16)
    total = jnp.dot(placing, upper, preferred_element_type=jnp.float32)
    return total + jnp.dot(placing, lower, preferred_element_type=jnp.float32)


def finish(total, stacked, orbitals, row_blocks):
    shaped = total.reshape(row_blocks, stacked, orbitals, BLOCK).transpose(1, 2, 0, 3)
    return shaped.reshape(stacked, orbitals, row_blocks * BLOCK).astype(jnp.bfloat16)


def local(coefs, direction, tiles, block_rows, block_cols, counts):
    slots = tiles.shape[1]
    orbitals = coefs.shape[0]
    row_blocks = coefs.shape[1] // BLOCK
    slot_ids = lax.iota(jnp.int32, slots)
    used = (slot_ids < counts[0, 0]).astype(jnp.bfloat16)
    tile_flat = tiles[0] * used[:, None]
    rows_local = block_rows[0]
    cols_global = block_cols[0]
    whole_coefs, whole_direction = (
        lax.all_gather(coefs, "row", axis=1, tiled=True),
        lax.all_gather(direction, "row", axis=1, tiled=True),
    )
    all_blocks = whole_coefs.shape[1] // BLOCK
    coef_panel = whole_coefs.reshape(1, orbitals, all_blocks, BLOCK)
    direction_panel = whole_direction.reshape(1, orbitals, all_blocks, BLOCK)
    both_panels = jnp.concatenate([coef_panel, direction_panel], axis=0)
    start_both = jnp.zeros((row_blocks, 2 * orbitals * BLOCK), jnp.float32)
    total = make_folder(
        both_panels,
        row_blocks,
        start_both,
        (
            lax.all_gather(tile_flat, "col", axis=0, tiled=True),
            lax.all_gather(rows_local, "col", axis=0, tiled=True),
            lax.all_gather(cols_global, "col", axis=0, tiled=True),
        ),
    )
    result = finish(total, 2, orbitals, row_blocks)
    return (result[0], result[1])


def solution(mesh):
    return jax.shard_map(
        local,
        mesh=mesh,
        in_specs=(
            P("col", "row"),
            P("col", "row"),
            P("row", "col", None),
            P("row", "col"),
            P("row", "col"),
            P("row", "col"),
        ),
        out_specs=(P("col", "row"), P("col", "row")),
        check_vma=False,
    )
```

profile of v0, /device:TPU:0, one launch (start us, length us, event | category | flops | bytes accessed | tf_op | source)
XLA Modules:
  0.0 150.9 jit_solution(13641684130491760249)
XLA Ops:
  7.2 1.8 %copy.19 = bf16[128,1024]{0,1:T(8,128)(2,1)} copy(bf16[128,1024]{1,0:T(8,128)(2,1)} %param.6) | data formatting | bytes 524288 | tf_op args[0]
  9.1 1.8 %copy.20 = bf16[128,1024]{0,1:T(8,128)(2,1)} copy(bf16[128,1024]{1,0:T(8,128)(2,1)} %param.7) | data formatting | bytes 524288 | tf_op args[1]
  11.6 1.7 %bitcast_multiply_fusion = bf16[24,4096]{1,0:T(8,128)(2,1)} fusion(bf16[1,24,4096]{2,1,0:T(8,128)(2,1)} %param.8, bf16[24]{0:T(256)(128)(2,1)S(1)} %compare_convert_fusion), kind=kLoop, calls=%fused_computation.12 | loop fusion | flops 98304 | bytes 393264 | tf_op jit(solution)/shard_map/mul | solution.py:35
  13.3 1.2 dynamic-slice
  15.1 0.8 bitcast_dynamic-update-slice_fusion
  15.9 0.7 bitcast_dynamic-update-slice_fusion.1
  16.6 13.1 %all-reduce.2 = (s32[192]{0:T(256)S(1)}, s32[192]{0:T(256)S(1)}) all-reduce(s32[192]{0:T(256)S(1)} %bitcast_dynamic-update-slice_fusion, s32[192]{0:T(256)S(1)} %bitcast_dynamic-update-slice_fusion.1), channel_id=3, replica_groups=mesh['row'=4,'col'=8] {'col'}, use_global_device_ids=true, to_apply=%add.1 | all-reduce | flops 384 | bytes 3072 | tf_op jit(solution)/shard_map/all_gather | solution.py:54
  29.7 18.8 %all-gather.8.cloned.1.call-done = bf16[128,4096]{0,1:T(8,128)(2,1)} async-done(((bf16[128,1024]{0,1:T(8,128)(2,1)}), bf16[128,4096]{0,1:T(8,128)(2,1)}) %all-gather.8.cloned.1.call-update) | async-done | bytes 1048592 | tf_op jit(solution)/shard_map/all_gather | solution.py:40
  48.5 1.7 %pad_maximum_fusion = bf16[2,128,64,64]{1,3,2,0:T(8,128)(2,1)S(1)} fusion(bf16[1,128,64,64]{1,3,2,0:T(8,128)(2,1)} %bitcast.34, bf16[1,128,64,64]{1,3,2,0:T(8,128)(2,1)} %bitcast.33), kind=kLoop, calls=%fused_computation.11 | loop fusion | flops 1048576 | bytes 4194304 | tf_op jit(solution)/shard_map/concatenate | solution.py:45
  50.2 8.1 %gather_fusion = bf16[192,2,128,64]{2,3,1,0:T(8,128)(2,1)} fusion(bf16[2,128,64,64]{1,3,2,0:T(8,128)(2,1)S(1)} %pad_maximum_fusion, s32[1024]{0:T(1024)S(1)} %pad_clamp_fusion), kind=kCustom, calls=%fused_computation | custom fusion | bytes 12583680 | tf_op jit(solution)/shard_map/jit(_take)/gather | solution.py:14
  58.3 36.6 %all-gather.10.cloned.1.call-done = bf16[192,4096]{1,0:T(8,128)(2,1)} async-done(((bf16[24,4096]{1,0:T(8,128)(2,1)}), bf16[192,4096]{1,0:T(8,128)(2,1)}) %all-gather.10.cloned.1.call-update) | async-done | bytes 1572880 | tf_op jit(solution)/shard_map/all_gather | solution.py:52
  94.9 3.9 %copy.21 = bf16[192,4096]{0,1:T(8,128)(2,1)} copy(bf16[192,4096]{1,0:T(8,128)(2,1)} %all-gather.10.cloned.1.call-done) | data formatting | bytes 3145728 | tf_op jit(solution)/shard_map/all_gather | solution.py:52
  98.8 4.2 %copy.28 = bf16[192,64,64,1]{2,1,3,0:T(8,128)(2,1)S(1)} copy(bf16[192,64,64,1]{0,2,1,3:T(8,128)(2,1)} %bitcast.29) | data formatting | bytes 3145728 | tf_op jit(solution)/shard_map/reshape | solution.py:13
  103.0 9.2 %fusion.2 = f32[192,2,128,64]{2,3,1,0:T(8,128)} fusion(bf16[192,64,64,1]{2,1,3,0:T(8,128)(2,1)S(1)} %copy.28, bf16[192,2,128,64]{2,3,1,0:T(8,128)(2,1)} %gather_fusion, pred[192]{0:T(512)(128)(4,1)S(1)} %compare_and_fusion), kind=kOutput, calls=%fused_computation.6 | convolution fusion | flops 405798912 | bytes 20447424 | tf_op jit(solution)/shard_map/pij,sopj->psoi/dot_general | solution.py:15
  112.2 17.3 %copy.23 = f32[192,2,128,64]{0,3,2,1:T(8,128)} copy(f32[192,2,128,64]{2,3,1,0:T(8,128)} %fusion.2) | data formatting | bytes 25165824 | tf_op jit(solution)/shard_map/pij,sopj->psoi/dot_general | solution.py:15
  129.6 6.9 %fusion.1 = (bf16[192,16384]{0,1:T(8,128)(2,1)S(1)}, bf16[192,16384]{0,1:T(8,128)(2,1)S(1)}) fusion(f32[192,2,128,64]{0,3,2,1:T(8,128)} %copy.23), kind=kLoop, calls=%fused_computation.5 | loop fusion | flops 12582912 | bytes 25165824 | tf_op jit(solution)/shard_map/convert_element_type | solution.py:18
  136.4 2.3 %fusion.7 = f32[16,16384]{1,0:T(8,128)S(1)} fusion(bf16[192,16384]{0,1:T(8,128)(2,1)S(1)} %get-tuple-element.9, s32[192]{0:T(256)S(1)} %get-tuple-element.7), kind=kOutput, calls=%fused_computation.14 | convolution fusion | flops 100666368 | bytes 7340800 | tf_op jit(solution)/shard_map/dot_general | solution.py:20
  138.7 2.3 %fusion = bf16[16,16384]{1,0:T(8,128)(2,1)S(1)} fusion(f32[16,16384]{1,0:T(8,128)S(1)} %fusion.7, bf16[192,16384]{0,1:T(8,128)(2,1)S(1)} %get-tuple-element.8, s32[192]{0:T(256)S(1)} %get-tuple-element.7), kind=kOutput, calls=%fused_computation.2 | convolution fusion | flops 101190656 | bytes 7865088 | tf_op jit(solution)/shard_map/dot_general | solution.py:21
  141.0 1.1 convert_element_type.32
  142.1 0.1 fusion.11
  142.2 0.2 copy.25
  142.5 0.9 copy.27
  143.3 0.2 copy.24
  143.5 0.9 copy.26
  (13 shorter events, 0.2 us)
Async XLA Ops:
  7.2 22.6 %all-gather.6.cloned.1.call-start = ((), (), s32[]{:S(2)}) async-start(), calls=%async_computation | async-start | bytes 1310720 | tf_op jit(solution)/shard_map/all_gather | solution.py:39
  9.0 39.5 %all-gather.8.cloned.1.call-start = ((), (), s32[]{:S(2)}) async-start(), calls=%async_computation.1 | async-start | bytes 1310720 | tf_op jit(solution)/shard_map/all_gather | solution.py:40
  10.9 84.0 %all-gather.10.cloned.1.call-start = ((), (), s32[]{:S(2)}) async-start(), calls=%async_computation.2 | async-start | bytes 1769472 | tf_op jit(solution)/shard_map/all_gather | solution.py:52
Sparse Core Ops, SparseCore 0:
  10.1 19.4 all-gather.5
  31.7 16.7 all-gather.7
  50.7 44.1 all-gather.9
where the time goes:
time: 152 us; the launch traced here: 151 us
  waiting for transfers between devices  55.4 us (36%)
  local copies, waits for them, and re-layouts  43.2 us (28%)
  between operations  15 us (10%)
  matrix products  13.7 us (9%)
  blocking collectives  13.1 us (9%)
  other arithmetic  10.3 us (7%)
    all_gather x1, waiting for transfers between devices, local(): lax.all_gather(tile_flat, 'col', axis=0, tiled=True)  36.6 us
    all_gather x1, waiting for transfers between devices, local(): lax.all_gather(direction, 'row', axis=1, tiled=True)  18.8 us
    dot_general x1, local copies, waits for them, and re-layouts, make_folder(): jnp.einsum('pij,sopj->psoi', tile_mats, picked, preferred_element_type=jn...  17.3 us
    all_gather x1, blocking collectives, local(): lax.all_gather(cols_global, 'col', axis=0, tiled=True)  13.1 us
    dot_general x1, matrix products, make_folder(): jnp.einsum('pij,sopj->psoi', tile_mats, picked, preferred_element_type=jn...  9.17 us
    gather x1, local copies, waits for them, and re-layouts, make_folder(): picked = jnp.take(panels, tile_cols, axis=2)  8.09 us
    unnamed x9, local copies, waits for them, and re-layouts  8.02 us
    convert_element_type x1, other arithmetic, make_folder(): lower = (contrib - upper.astype(jnp.float32)).astype(jnp.bfloat16)  6.87 us
  transfers between devices with their start and end apart: 3, of which 2 were waited for; matrix products, arithmetic and copies ran while one was open for 11% of the time, Pallas kernels for 0%

commit v1 on v0

v1 whole, which is shorter than its diff:
```python
import functools

import jax
import jax.numpy as jnp
from jax import lax
from jax.experimental import pallas as pl
from jax.experimental.pallas import tpu as pltpu
from jax.sharding import PartitionSpec as P

BLOCK = 64
X_CHUNKS = 4
HALVES = 2
P_SLOTS = 5
MESH = pl.DeviceIdType.MESH


def kernel(n_row, n_col, coef, direc, tiles, rows, cols, counts, out_c, out_d,
           xall, tall, mall, smeta, pbuf, gbuf, acc,
           sib_s, sib_r, cross_s, cross_r, fwd_s, fwd_r, ring_s, ring_r, meta_s, meta_r, loc):
    orbs, basis = coef.shape
    width = 2 * orbs
    slots = rows.shape[1]
    blocks = basis // BLOCK
    half_rows = BLOCK // HALVES
    chips = n_row // 2
    steps = n_col // 2
    part = basis // X_CHUNKS
    per = part // BLOCK

    me_r, me_c = lax.axis_index("row"), lax.axis_index("col")
    chip, core = me_r // 2, me_r % 2
    sibling = chip * 2 + 1 - core
    turn = me_c % 2
    pos = me_c // 2 + turn * (n_col - 1 - 2 * (me_c // 2))

    def at_pos(p):
        side = p // steps
        return 2 * (p + side * (n_col - 1 - 2 * p)) + side

    nxt, prv = at_pos((pos + 1) % n_col), at_pos((pos + n_col - 1) % n_col)

    barrier = pltpu.get_barrier_semaphore()
    for c in (nxt, prv):
        pl.semaphore_signal(barrier, inc=1, device_id=(me_r, c), device_id_type=MESH)
    pl.semaphore_signal(barrier, inc=1, device_id=(sibling, me_c), device_id_type=MESH)
    for k in range(1, chips):
        pl.semaphore_signal(barrier, inc=1, device_id=(((chip + k) % chips) * 2 + core, me_c), device_id_type=MESH)

    ids = lax.broadcasted_iota(jnp.int32, (1, slots), 1)
    mall[0, 0:1, 0:slots] = jnp.where(ids < counts[0, 0], rows[...], -1)
    mall[0, 1:2, 0:slots] = cols[...]
    tall[0] = tiles[...]
    base = me_r * blocks
    for c in range(X_CHUNKS):
        for a, src in enumerate((coef, direc)):
            piece = src[:, c * part:(c + 1) * part].astype(jnp.float32).T.astype(jnp.bfloat16)
            xall[pl.ds(base + c * per, per), :, a * orbs:(a + 1) * orbs] = piece.reshape(per, BLOCK, orbs)
    pl.semaphore_wait(barrier, 2 + 1 + chips - 1)

    def x_ref(owner, c):
        return xall.at[pl.ds(owner * blocks + c * per, per)]

    def x_copy(owner, c, to, send, recv):
        return pltpu.make_async_remote_copy(
            src_ref=x_ref(owner, c), dst_ref=x_ref(owner, c), send_sem=send, recv_sem=recv,
            device_id=(to, me_c), device_id_type=MESH)

    def cross_to(k, c):
        return x_copy(me_r, c, ((chip + k) % chips) * 2 + core, cross_s.at[k - 1, c], cross_r.at[k - 1, c])

    def cross_from(k, c):
        owner = ((chip + chips - k) % chips) * 2 + core
        return x_copy(owner, c, owner, cross_s.at[k - 1, c], cross_r.at[k - 1, c])

    def sib_to(c):
        return x_copy(me_r, c, sibling, sib_s.at[c], sib_r.at[c])

    def sib_from(c):
        return x_copy(sibling, c, sibling, sib_s.at[c], sib_r.at[c])

    def fwd_to(k, c):
        owner = ((chip + chips - k) % chips) * 2 + core
        return x_copy(owner, c, sibling, fwd_s.at[k - 1, c], fwd_r.at[k - 1, c])

    def fwd_from(k, c):
        owner = ((chip + chips - k) % chips) * 2 + 1 - core
        return x_copy(owner, c, sibling, fwd_s.at[k - 1, c], fwd_r.at[k - 1, c])

    def ring_slots(d, t):
        return (t - 1, t) if d == 0 else ((n_col - t + 1) % n_col, n_col - t)

    def ring(d, t, h):
        a, b = ring_slots(d, t)
        cut = pl.ds(h * half_rows, half_rows)
        return pltpu.make_async_remote_copy(
            src_ref=tall.at[a, cut], dst_ref=tall.at[b, cut],
            send_sem=ring_s.at[d, t - 1, h], recv_sem=ring_r.at[d, t - 1, h],
            device_id=(me_r, nxt if d == 0 else prv), device_id_type=MESH)

    def meta(d, t):
        a, b = ring_slots(d, t)
        return pltpu.make_async_remote_copy(
            src_ref=mall.at[a], dst_ref=mall.at[b],
            send_sem=meta_s.at[d, t - 1], recv_sem=meta_r.at[d, t - 1],
            device_id=(me_r, nxt if d == 0 else prv), device_id_type=MESH)

    def ring_parts(t):
        if t < steps:
            return [(d, h) for h in range(HALVES) for d in (0, 1)], (0, 1)
        return [(0, 0), (1, 1)], (0,)

    def to_smem(slot):
        copy = pltpu.make_async_copy(mall.at[slot], smeta.at[slot], loc.at[slot])
        copy.start()
        copy.wait()

    lane = lax.broadcasted_iota(jnp.int32, (16, 2 * BLOCK), 1)

    def slot_of(q):
        return (q % 2) * ((q + 1) // 2) + (1 - q % 2) * ((n_col - q // 2) % n_col)

    def build(q):
        slot, place = slot_of(q), q % P_SLOTS

        def pair(i, carry):
            at = pl.ds(pl.multiple_of(i * 2 * BLOCK, 2 * BLOCK), 2 * BLOCK)
            mats = tall[slot, :, at].reshape(BLOCK // 16, 16, 2 * BLOCK)
            target = jnp.where(lane < BLOCK, smeta[slot, 0, 2 * i], smeta[slot, 0, 2 * i + 1])
            for b in range(blocks):
                keep = jnp.where(target == b, 1.0, 0.0).astype(jnp.bfloat16)
                pbuf[place, b * BLOCK:(b + 1) * BLOCK, at] = (mats * keep[None]).reshape(BLOCK, 2 * BLOCK)
            return carry

        lax.fori_loop(0, slots // 2, pair, 0)

    def compute(q):
        slot, place = slot_of(q), q % P_SLOTS

        def pick(s, carry):
            gbuf[s] = xall[smeta[slot, 1, s]]
            return carry

        lax.fori_loop(0, slots, pick, 0, unroll=4)

        def strip(m, carry):
            at = pl.ds(pl.multiple_of(m * 256, 256), 256)
            acc[at, :] += jnp.dot(pbuf[place, at, :], gbuf[...].reshape(slots * BLOCK, width), preferred_element_type=jnp.float32)
            return carry

        lax.fori_loop(0, basis // 256, strip, 0)

    def send_ring(t):
        pieces, metas = ring_parts(t)
        for d in metas:
            meta(d, t).start()
        for d, h in pieces:
            ring(d, t, h).start()

    def ring_event(t):
        pieces, metas = ring_parts(t)
        more, more_metas = ring_parts(t + 1) if t < steps else ((), ())
        for d in metas:
            meta(d, t).wait_recv()
            if d in more_metas:
                meta(d, t + 1).start()
        for d, h in pieces:
            ring(d, t, h).wait_recv()
            if (d, h) in more:
                ring(d, t + 1, h).start()
        for d in metas:
            to_smem(ring_slots(d, t)[1])

    for c in range(X_CHUNKS):
        for k in range(1, chips):
            cross_to(k, c).start()
        if c == 0:
            send_ring(1)
    for c in range(X_CHUNKS):
        sib_to(c).start()
    to_smem(0)
    acc[...] = jnp.zeros_like(acc)
    build(0)

    events = [(((k - 1) * X_CHUNKS + c + 1) * 2.6, 0, k, c) for k in range(1, chips) for c in range(X_CHUNKS)]
    events += [(t * 3.9, 1, t, 0) for t in range(1, steps)]
    for _, kind, k, c in sorted(events):
        if kind == 0:
            cross_from(k, c).wait_recv()
            fwd_to(k, c).start()
        else:
            ring_event(k)
            for q in (2 * k - 1, 2 * k):
                if q < P_SLOTS:
                    build(q)
    for c in range(X_CHUNKS):
        sib_from(c).wait_recv()
    for k in range(1, chips):
        for c in range(X_CHUNKS):
            fwd_from(k, c).wait_recv()

    def early(q, carry):
        compute(q)
        return carry

    def late(q, carry):
        build(q)
        compute(q)
        return carry

    lax.fori_loop(0, P_SLOTS, early, 0)
    lax.fori_loop(P_SLOTS, n_col - 1, late, 0)
    ring_event(steps)
    lax.fori_loop(n_col - 1, n_col, late, 0)

    for a, out in enumerate((out_c, out_d)):
        for m in range(basis // 256):
            out[:, m * 256:(m + 1) * 256] = acc[m * 256:(m + 1) * 256, a * orbs:(a + 1) * orbs].T.astype(jnp.bfloat16)

    for c in range(X_CHUNKS):
        sib_to(c).wait_send()
        for k in range(1, chips):
            cross_to(k, c).wait_send()
            fwd_to(k, c).wait_send()
    for t in range(1, steps + 1):
        pieces, metas = ring_parts(t)
        for d in metas:
            meta(d, t).wait_send()
        for d, h in pieces:
            ring(d, t, h).wait_send()


def local(n_row, n_col, coefs, direction, tiles, block_rows, block_cols, counts):
    slots = tiles.shape[1]
    orbs, basis = coefs.shape
    width = 2 * orbs
    tile_mats = tiles[0].reshape(slots, BLOCK, BLOCK).transpose(1, 0, 2).reshape(BLOCK, slots * BLOCK)
    chips, steps = n_row // 2, n_col // 2
    vmem = pl.BlockSpec(memory_space=pltpu.VMEM)
    dma = pltpu.SemaphoreType.DMA
    out = jax.ShapeDtypeStruct((orbs, basis), jnp.bfloat16)
    return pl.pallas_call(
        functools.partial(kernel, n_row, n_col),
        out_shape=(out, out),
        in_specs=[vmem] * 5 + [pl.BlockSpec(memory_space=pltpu.SMEM)],
        out_specs=(vmem, vmem),
        scratch_shapes=[
            pltpu.VMEM((n_row * basis // BLOCK, BLOCK, width), jnp.bfloat16),
            pltpu.VMEM((n_col, BLOCK, slots * BLOCK), jnp.bfloat16),
            pltpu.VMEM((n_col, 8, 128), jnp.int32),
            pltpu.SMEM((n_col, 8, 128), jnp.int32),
            pltpu.VMEM((P_SLOTS, basis, slots * BLOCK), jnp.bfloat16),
            pltpu.VMEM((slots, BLOCK, width), jnp.bfloat16),
            pltpu.VMEM((basis, width), jnp.float32),
            dma((X_CHUNKS,)), dma((X_CHUNKS,)),
            dma((chips - 1, X_CHUNKS)), dma((chips - 1, X_CHUNKS)),
            dma((chips - 1, X_CHUNKS)), dma((chips - 1, X_CHUNKS)),
            dma((2, steps, HALVES)), dma((2, steps, HALVES)),
            dma((2, steps)), dma((2, steps)),
            dma((n_col,)),
        ],
        compiler_params=pltpu.CompilerParams(
            collective_id=0, has_side_effects=True, vmem_limit_bytes=56 * 2**20),
        name="block_sparse_apply",
    )(coefs, direction, tile_mats, block_rows, block_cols, counts)


def solution(mesh):
    body = functools.partial(local, mesh.shape["row"], mesh.shape["col"])
    return jax.shard_map(
        body,
        mesh=mesh,
        in_specs=(
            P("col", "row"),
            P("col", "row"),
            P("row", "col", None),
            P("row", "col"),
            P("row", "col"),
            P("row", "col"),
        ),
        out_specs=(P("col", "row"), P("col", "row")),
        check_vma=False,
    )
```

time: 152 us -> 45.9 us (0.30)
  waiting for transfers between devices: 55.4 us -> 0 us
  Pallas kernels: 0 us -> 39.5 us
  local copies, waits for them, and re-layouts: 43.2 us -> 4.95 us
  matrix products: 13.7 us -> 0 us
  between operations: 15 us -> 1.31 us
  blocking collectives: 13.1 us -> 0 us
  other arithmetic: 10.3 us -> 0 us
    all_gather x3 -> x0, waiting for transfers between devices: 55.4 us -> none  [the longest x1 36.6 us: local(): lax.all_gather(tile_flat, 'col', axis=0, tiled=True)]
    pallas_call x0 -> x1, Pallas kernels: none -> 39.5 us  [local(): pl.pallas_call(functools.partial(kernel, n_row, n_col), out_shape=(out, o...]
    dot_general x1 -> x0, local copies, waits for them, and re-layouts: 17.3 us -> none  [make_folder(): jnp.einsum('pij,sopj->psoi', tile_mats, picked, preferred_element_type=jn...]
    dot_general x3 -> x0, matrix products: 13.7 us -> none  [the longest x1 9.17 us: make_folder(): jnp.einsum('pij,sopj->psoi', tile_mats, picked, preferred_element_type=jn...]
    all_gather x1 -> x0, blocking collectives: 13.1 us -> none  [local(): lax.all_gather(cols_global, 'col', axis=0, tiled=True)]
    gather x1 -> x0, local copies, waits for them, and re-layouts: 8.09 us -> none  [make_folder(): picked = jnp.take(panels, tile_cols, axis=2)]
    convert_element_type x2 -> x0, other arithmetic: 6.87 us -> none  [the longest x1 6.87 us: make_folder(): lower = (contrib - upper.astype(jnp.float32)).astype(jnp.bfloat16)]
    unnamed x9 -> x4, local copies, waits for them, and re-layouts: 8.02 us -> 2.42 us
  transfers between devices with their start and end apart: 3 -> 0, of which waited for: 2 -> 0; matrix products, arithmetic and copies ran while one was open for 11% -> 0% of each run, Pallas kernels for 0% -> 0%
where the time goes in v1:
time: 45.9 us; the launch traced here: 45.7 us
  Pallas kernels  39.5 us (86%)
  local copies, waits for them, and re-layouts  4.95 us (11%)
  between operations  1.31 us (3%)
    pallas_call x1, Pallas kernels, local(): pl.pallas_call(functools.partial(kernel, n_row, n_col), out_shape=(out, o...  39.5 us
    unnamed x4, local copies, waits for them, and re-layouts  2.42 us
    another operation x2, local copies, waits for them, and re-layouts, local(): tiles[0].reshape(slots, BLOCK, BLOCK).transpose(1, 0, 2)  1.59 us
    reshape x1, local copies, waits for them, and re-layouts, local(): tiles[0].reshape(slots, BLOCK, BLOCK).transpose(1, 0, 2)  0.94 us

profile of v1, /device:TPU:0, one launch (start us, length us, event | category | flops | bytes accessed | tf_op | source)
XLA Modules:
  0.0 45.7 jit_solution(12080788118369556751)
XLA Ops:
  0.6 1.3 %reshape_squeeze.3 = bf16[24,64,64]{2,1,0:T(8,128)(2,1)S(1)} reshape(bf16[1,24,4096]{2,1,0:T(8,128)(2,1)} %param.8) | data formatting | bytes 393216 | tf_op jit(solution)/shard_map/reshape;squeeze | solution.py:236
  2.0 0.3 copy.10
  2.2 0.9 %reshape.7.tiles = bf16[64,1536]{1,0:T(8,128)(2,1)} reshape(bf16[64,24,64]{2,1,0:T(8,128)(2,1)S(1)} %bitcast.3) | data formatting | bytes 393216 | tf_op jit(solution)/shard_map/reshape | solution.py:236
  3.8 39.5 %block_sparse_apply.1 = (bf16[128,1024]{1,0:T(8,128)(2,1)}, bf16[128,1024]{1,0:T(8,128)(2,1)}) custom-call(bf16[128,1024]{1,0:T(8,128)(2,1)} %coef.1, bf16[128,1024]{1,0:T(8,128)(2,1)} %direc.1, bf16[64,1536]{1,0:T(8,128)(2,1)} %reshape.7.tiles, s32[1,24]{1,0:T(1,128)} %rows.1, s32[1,24]{1,0:T(1,128)} %cols.1, s32[1,1]{1,0:T(1,128)S(6)} %copy.13.counts), custom_call_target="tpu_custom_call" | custom-call | tf_op jit(solution)/shard_map/block_sparse_apply/pallas_call | solution.py:241
  43.3 0.0 copy-start
  43.3 1.7 %copy.14 = bf16[128,1024]{1,0:T(8,128)(2,1)} copy(bf16[128,1024]{1,0:T(8,128)(2,1)} %get-tuple-element.4) | data formatting | bytes 524288
  45.0 0.0 copy-done
  45.0 0.7 %copy.15 = bf16[128,1024]{1,0:T(8,128)(2,1)} copy(bf16[128,1024]{1,0:T(8,128)(2,1)S(1)} %copy-done) | data formatting | bytes 524288
Async XLA Ops:
  43.3 1.7 %copy-start = (bf16[128,1024]{1,0:T(8,128)(2,1)S(1)}, bf16[128,1024]{1,0:T(8,128)(2,1)}, u32[]{:S(2)}) copy-start(bf16[128,1024]{1,0:T(8,128)(2,1)} %get-tuple-element.5) | copy-start | bytes 786436
